TPU v7x, 32 devices: a whole 2x2x4 slice. The times are simulated.
32 devices in a mesh: dom: 8 (over z, x), rep: 4 (over y, core).
Axes of the slice: x: 2, y: 2, z: 4, core: 2. Of those that a mesh axis runs over, the one named last changes fastest.
Arguments:
- embeddings: float32 [262144, 256], P(('dom', 'rep')), may hold values from -1.5 to 1.5
- row_state: float32 [262144], P(('dom', 'rep')), may hold values from 0.01 to 0.1
- relations: float32 [64, 256], replicated, may hold values from 0.1 to 1.9
- rel_state: float32 [64, 256], replicated, may hold values from 2 to 40
- edge_src: int32 [8, 4, 2, 4, 1000], P('dom', 'rep'), may hold values from 0 to 8191
- edge_dst: int32 [8, 4, 2, 4, 1000], P('dom', 'rep'), may hold values from 0 to 8191
- edge_rel: int32 [8, 4, 2, 4, 1000], P('dom', 'rep'), may hold values from 0 to 63
- batch_count: int32 [8, 4, 2], P('dom', 'rep'), may hold values from 1 to 4, as said below
Outputs:
- new_embeddings: float32 [262144, 256], P(('dom', 'rep'))
- new_row_state: float32 [262144], P(('dom', 'rep'))
- new_relations: float32 [64, 256], replicated
- new_rel_state: float32 [64, 256], replicated
Inputs may be any that keep to these rules, and one draw needn't show every extreme that they name: `batch_count`: batches at or past the count are ignored; some bucket of each round set reaches 4.
All inputs are finite; a program needn't handle non-finite values.
Results may differ from a plain program's by a relative error of at most 0.0031.
Values may be sent and summed in bfloat16 or wider, within the bound.
No kernel may reach another device: no remote copies, remote signals or barrier semaphores. Data moves between devices by JAX's collectives and lax.ppermute only.
A program may use at most 128 MiB of HBM per device.

v0:
```python
import jax
import jax.numpy as jnp
from jax import lax
from jax.sharding import PartitionSpec as P

ROUNDS = 2


learn_rate = 0.1
rel_rate = 0.1


def from_partner(shard, axis, distance):
    return lax.ppermute(shard, axis, [(i, i ^ 1 << distance) for i in range(lax.axis_size(axis))])


def batch_terms(source_rows, target_rows, kind_index, relations):
    rel_count = relations.shape[0]
    onehot = (kind_index[:, None] == jnp.arange(rel_count, dtype=jnp.int32)[None, :]).astype(
        relations.dtype
    )
    diagonal = jnp.dot(onehot, relations, precision=lax.Precision.HIGHEST)
    source_full = source_rows.astype(relations.dtype)
    queries = (source_full * diagonal).astype(jnp.bfloat16)
    scores = lax.dot_general(
        queries, target_rows, (((1,), (1,)), ((), ())), preferred_element_type=jnp.float32
    )
    size_rows = scores.shape[0]
    on_diag = jnp.arange(size_rows)[:, None] == jnp.arange(size_rows)[None, :]
    probs = jax.nn.sigmoid(scores)
    weights_bf = jnp.where(on_diag, probs - 1.0, probs / (size_rows - 1)).astype(jnp.bfloat16)
    grad_query = jnp.dot(weights_bf, target_rows, preferred_element_type=jnp.float32)
    grad_target = lax.dot_general(
        weights_bf, queries, (((0,), (0,)), ((), ())), preferred_element_type=jnp.float32
    )
    grad_source = grad_query * diagonal
    grad_rel = lax.dot_general(
        onehot, grad_query * source_full, (((0,), (0,)), ((), ())), precision=lax.Precision.HIGHEST
    )
    return (grad_source, grad_target, grad_rel)


def on_device(
    embeddings, row_state, relations, rel_state, edge_src, edge_dst, edge_rel, batch_count
):
    bit_count = lax.axis_size("dom").bit_length() - 1
    row_count, row_width = embeddings.shape
    for number in range(ROUNDS):
        swap_bit = bit_count - 1 - number
        own_rows = embeddings.astype(jnp.bfloat16)
        source_index = edge_src[0, 0, number]
        target_index = edge_dst[0, 0, number]
        kind_table = edge_rel[0, 0, number]
        live_batches = batch_count[0, 0, number]
        empty_grad = jnp.zeros((row_count, row_width), jnp.float32)
        empty_rel = jnp.zeros(relations.shape, jnp.float32)
        slot_count, batch_size = source_index.shape
        sent_rows = jnp.take(own_rows, source_index.reshape(-1), axis=0).reshape(
            slot_count, batch_size, row_width
        )
        got_rows = from_partner(sent_rows, "dom", swap_bit)
        got_ids, got_live = from_partner(
            (jnp.stack([target_index, kind_table], axis=1), live_batches), "dom", swap_bit
        )

        def serve_step(batch_number, inner_carry):
            own_grad, edge_grad, rel_grad = inner_carry
            targets = got_ids[batch_number, 0]
            source_grad, target_grad, kind_grad = batch_terms(
                got_rows[batch_number],
                jnp.take(own_rows, targets, axis=0),
                got_ids[batch_number, 1],
                relations,
            )
            return (
                own_grad.at[targets].add(target_grad),
                edge_grad.at[batch_number].set(source_grad),
                rel_grad + kind_grad,
            )

        empty_edges = jnp.zeros((slot_count, batch_size, row_width), jnp.float32)
        own_grad, edge_grad, rel_grad = lax.fori_loop(
            0, got_live, serve_step, (empty_grad, empty_edges, empty_rel)
        )
        returned = from_partner(edge_grad, "dom", swap_bit)
        row_grad = own_grad.at[source_index.reshape(-1)].add(returned.reshape(-1, row_width))
        row_state = row_state + jnp.mean(row_grad * row_grad, axis=-1)
        embeddings = embeddings - learn_rate * row_grad / jnp.sqrt(row_state)[:, None]
        rel_total = lax.psum(rel_grad, ("dom", "rep"))
        rel_state = rel_state + rel_total * rel_total
        relations = relations - rel_rate * rel_total / jnp.sqrt(rel_state)
    return (embeddings, row_state, relations, rel_state)


def solution(mesh):
    return jax.shard_map(
        on_device,
        mesh=mesh,
        in_specs=(
            P(("dom", "rep"), None),
            P(("dom", "rep")),
            P(),
            P(),
            P("dom", "rep", None, None, None),
            P("dom", "rep", None, None, None),
            P("dom", "rep", None, None, None),
            P("dom", "rep", None),
        ),
        out_specs=(P(("dom", "rep"), None), P(("dom", "rep")), P(), P()),
        check_vma=False,
    )
```

profile of v0, /device:TPU:6, one launch (start us, length us, event | category | flops | bytes accessed | tf_op | source)
XLA Modules:
  0.0 844.6 jit_solution(12285081923085452981)
XLA Ops:
  8.1 5.8 convert_element_type.50
  13.9 16.0 %gather_fusion.2 = bf16[4000,256]{1,0:T(8,128)(2,1)S(1)} fusion(bf16[8192,256]{1,0:T(8,128)(2,1)} %convert_element_type.50, s32[4096]{0:T(1024)S(1)} %pad_clamp_fusion.3), kind=kCustom, calls=%fused_computation.clone | custom fusion | bytes 4112000 | tf_op jit(solution)/shard_map/jit(_take)/gather | solution.py:58
  29.9 3.0 broadcast_select_fusion.7
  33.0 2.6 collective-permute-start.2
  36.7 2.6 collective-permute-start
  39.2 86.5 %collective-permute-done = s32[]{:T(128)} collective-permute-done((s32[]{:T(128)}, s32[]{:T(128)}, u32[]{:S(2)}, u32[]{:S(2)}) %collective-permute-start) | collective-permute-done | bytes 36 | tf_op jit(solution)/shard_map/ppermute | solution.py:14
  125.7 2.3 broadcast.203.clone
  128.0 3.8 broadcast.202.clone
  131.8 31.8 %while.34 = (s32[]{:T(128)}, f32[8192,256]{1,0:T(8,128)}, f32[4,1000,256]{2,1,0:T(8,128)}, f32[64,256]{1,0:T(8,128)S(1)}, s32[]{:T(128)}, /*index=5*/s32[4,2,100...) while((s32[]{:T(128)}, f32[8192,256]{1,0:T(8,128)}, ...), condition=%wide.region_3.6_spmd, body=%wide.region_0.5_spmd.sunk | while | flops 1939933440 | bytes 21105448 | solution.py:82
  132.5 0.8 and_reduce_fusion.4
  133.3 6.3 gather_fusion
  139.7 1.7 fusion.62
  141.4 2.2 select_convert_fusion.4
  143.6 0.9 fusion.63
  144.5 3.8 fusion.64
  148.3 1.8 convolution_add_fusion.4
  150.1 12.6 %scatter_fusion = f32[8192,256]{1,0:T(8,128)} fusion(f32[8192,256]{1,0:T(8,128)} %get-tuple-element.487, s32[1000]{0:T(1024)S(1)} %bitcast.120, f32[1000,256]{1,0:T(8,128)S(1)} %fusion.63), kind=kCustom, calls=%fused_computation.4.clone.1 | custom fusion | flops 256000 | bytes 3076000 | tf_op jit(solution)/shard_map/while/body/scatter-add | solution.py:76
  163.9 163.9 %collective-permute-done.3 = f32[4,1000,256]{2,1,0:T(8,128)} collective-permute-done((f32[4,1000,256]{2,1,0:T(8,128)}, f32[4,1000,256]{2,1,0:T(8,128)}, u32[]{:S(2)}, u32[]{:S(2)}) %collective-permute-start.3) | collective-permute-done | bytes 4096032 | tf_op jit(solution)/shard_map/ppermute | solution.py:14
  327.8 29.4 %scatter_fusion.2 = f32[8192,256]{1,0:T(8,128)} fusion(f32[8192,256]{1,0:T(8,128)} %get-tuple-element.266, s32[4000]{0:T(1024)S(1)} %bitcast.123, f32[4000,256]{1,0:T(8,128)} %bitcast.21), kind=kCustom, calls=%fused_computation.6 | custom fusion | flops 1024000 | bytes 12304000 | tf_op jit(solution)/shard_map/scatter-add | solution.py:86
  357.3 4.7 multiply_reduce_fusion.1
  362.0 1.1 copy-done
  363.0 5.4 fusion.23
  368.4 16.0 %gather_fusion.3 = bf16[4000,256]{1,0:T(8,128)(2,1)S(1)} fusion(bf16[8192,256]{1,0:T(8,128)(2,1)} %fusion.23, s32[4096]{0:T(1024)S(1)} %pad_clamp_fusion.2), kind=kCustom, calls=%fused_computation.2.clone | custom fusion | bytes 4112000 | tf_op jit(solution)/shard_map/jit(_take)/gather | solution.py:58
  384.5 3.0 broadcast_select_fusion.6
  387.5 14.2 %collective-permute-start.6 = (bf16[4,1000,256]{2,1,0:T(8,128)(2,1)}, bf16[4,1000,256]{2,1,0:T(8,128)(2,1)}, u32[]{:S(2)}, u32[]{:S(2)}) collective-permute-start(bf16[4,1000,256]{2,1,0:T(8,128)(2,1)} %bitcast.25), channel_id=1, source_target_pairs={{0,8},{4,12},{8,0},{12,4},{16,24},{20,28},{24,16},{28,20},{1,9},{5... | collective-permute-start | bytes 6144008 | tf_op jit(solution)/shard_map/ppermute | solution.py:14
  401.9 2.1 collective-permute-start.5
  403.9 136.0 %all-reduce.3.cloned.1.call-done = f32[64,256]{1,0:T(8,128)} async-done(((f32[64,256]{1,0:T(8,128)}), f32[64,256]{1,0:T(8,128)}) %all-reduce.3.cloned.1.call-update) | async-done | bytes 65552 | tf_op jit(solution)/shard_map/psum | solution.py:89
  539.9 0.9 multiply_subtract_fusion.1
  540.8 2.3 broadcast.203
  543.1 3.9 broadcast.202
  547.0 124.8 %while.35 = (s32[]{:T(128)}, f32[8192,256]{1,0:T(8,128)}, f32[4,1000,256]{2,1,0:T(8,128)}, f32[64,256]{1,0:T(8,128)S(1)}, s32[]{:T(128)}, /*index=5*/s32[4,2,100...) while((s32[]{:T(128)}, f32[8192,256]{1,0:T(8,128)}, ...), condition=%wide.region_10.13_spmd, body=%wide.region_7.12_spmd.sunk | while | flops 1939933440 | bytes 21105448 | solution.py:82
  548.7 6.3 gather_fusion.1
  555.1 1.7 fusion.70
  556.8 2.2 select_convert_fusion.5
  559.0 0.9 fusion.71
  559.9 3.8 fusion.72
  563.7 1.8 convolution_add_fusion.5
  565.5 12.8 %scatter_fusion.1 = f32[8192,256]{1,0:T(8,128)} fusion(f32[8192,256]{1,0:T(8,128)} %get-tuple-element.529, s32[1000]{0:T(1024)S(1)} %bitcast.121, f32[1000,256]{1,0:T(8,128)S(1)} %fusion.71), kind=kCustom, calls=%fused_computation.5.clone.1 | custom fusion | flops 256000 | bytes 3076000 | tf_op jit(solution)/shard_map/while/body/scatter-add | solution.py:76
  579.8 6.3 gather_fusion.1
  586.1 1.7 fusion.70
  587.8 2.2 select_convert_fusion.5
  590.0 0.9 fusion.71
  590.9 3.7 fusion.72
  594.6 1.8 convolution_add_fusion.5
  596.5 12.8 %scatter_fusion.1 = f32[8192,256]{1,0:T(8,128)} fusion(f32[8192,256]{1,0:T(8,128)} %get-tuple-element.529, s32[1000]{0:T(1024)S(1)} %bitcast.121, f32[1000,256]{1,0:T(8,128)S(1)} %fusion.71), kind=kCustom, calls=%fused_computation.5.clone.1 | custom fusion | flops 256000 | bytes 3076000 | tf_op jit(solution)/shard_map/while/body/scatter-add | solution.py:76
  610.7 6.3 gather_fusion.1
  617.0 1.7 fusion.70
  618.7 2.2 select_convert_fusion.5
  621.0 0.9 fusion.71
  621.8 3.7 fusion.72
  625.6 1.8 convolution_add_fusion.5
  627.4 12.8 %scatter_fusion.1 = f32[8192,256]{1,0:T(8,128)} fusion(f32[8192,256]{1,0:T(8,128)} %get-tuple-element.529, s32[1000]{0:T(1024)S(1)} %bitcast.121, f32[1000,256]{1,0:T(8,128)S(1)} %fusion.71), kind=kCustom, calls=%fused_computation.5.clone.1 | custom fusion | flops 256000 | bytes 3076000 | tf_op jit(solution)/shard_map/while/body/scatter-add | solution.py:76
  641.7 6.3 gather_fusion.1
  648.0 1.7 fusion.70
  649.7 2.2 select_convert_fusion.5
  651.9 0.9 fusion.71
  652.8 3.7 fusion.72
  656.5 1.8 convolution_add_fusion.5
  658.4 12.8 %scatter_fusion.1 = f32[8192,256]{1,0:T(8,128)} fusion(f32[8192,256]{1,0:T(8,128)} %get-tuple-element.529, s32[1000]{0:T(1024)S(1)} %bitcast.121, f32[1000,256]{1,0:T(8,128)S(1)} %fusion.71), kind=kCustom, calls=%fused_computation.5.clone.1 | custom fusion | flops 256000 | bytes 3076000 | tf_op jit(solution)/shard_map/while/body/scatter-add | solution.py:76
  672.5 118.7 %all-reduce.5.cloned.1.call-done = f32[64,256]{1,0:T(8,128)} async-done(((f32[64,256]{1,0:T(8,128)}), f32[64,256]{1,0:T(8,128)}) %all-reduce.5.cloned.1.call-update) | async-done | bytes 65552 | tf_op jit(solution)/shard_map/psum | solution.py:89
  791.2 1.5 multiply_subtract_fusion
  792.7 29.6 %scatter_fusion.3 = f32[8192,256]{1,0:T(8,128)} fusion(f32[8192,256]{1,0:T(8,128)} %get-tuple-element.269, s32[4000]{0:T(1024)S(1)} %bitcast.122, f32[4000,256]{1,0:T(8,128)} %bitcast.27), kind=kCustom, calls=%fused_computation.7 | custom fusion | flops 1024000 | bytes 12304000 | tf_op jit(solution)/shard_map/scatter-add | solution.py:86
  822.3 4.7 multiply_reduce_fusion
  828.0 9.7 %divide_subtract_fusion = f32[8192,256]{1,0:T(8,128)} fusion(f32[8192,256]{1,0:T(8,128)S(1)} %copy-done.1, f32[8192]{0:T(1024)S(1)} %get-tuple-element.314, f32[8192,256]{1,0:T(8,128)} %param.20, f32[8192]{0:T(1024)S(1)} %fusion.22, f32[8192,256]{1,0:T(8,128)} %scatter_fusion.2), kind=kLoop, calls=%fused_computation.60 | loop fusion | flops 12582912 | bytes 33619968 | tf_op jit(solution)/shard_map/sub | solution.py:88
  (90 shorter events, 7.2 us)
Async XLA Ops:
  7.2 532.8 %all-reduce.3.cloned.1.call-start = ((), (), s32[]{:S(2)}) async-start(), calls=%async_computation | async-start | bytes 131072 | tf_op jit(solution)/shard_map/psum | solution.py:89
  29.9 5.7 copy-start.9
  29.9 5.7 copy-start.10
  29.9 6.1 copy-start.11
  33.0 92.8 %collective-permute-start.2 = (bf16[4,1000,256]{2,1,0:T(8,128)(2,1)}, bf16[4,1000,256]{2,1,0:T(8,128)(2,1)}, u32[]{:S(2)}, u32[]{:S(2)}) collective-permute-start(bf16[4,1000,256]{2,1,0:T(8,128)(2,1)} %bitcast.19), channel_id=1, source_target_pairs={{0,16},{4,20},{8,24},{12,28},{16,0},{20,4},{24,8},{28,12},{1,17},{... | collective-permute-start | bytes 6144008 | tf_op jit(solution)/shard_map/ppermute | solution.py:14
  35.7 90.1 %collective-permute-start.1 = (s32[4,2,1000]{2,1,0:T(2,128)S(1)}, s32[4,2,1000]{2,1,0:T(2,128)S(1)}, u32[]{:S(2)}, u32[]{:S(2)}) collective-permute-start(s32[4,2,1000]{2,1,0:T(2,128)S(1)} %pad_add_fusion), channel_id=1, source_target_pairs={{0,16},{4,20},{8,24},{12,28},{16,0},{20,4},{24,8},{28,12},{1,17},{... | collective-permute-start | bytes 96008 | tf_op jit(solution)/shard_map/ppermute | solution.py:14
  36.7 89.1 %collective-permute-start = (s32[]{:T(128)}, s32[]{:T(128)}, u32[]{:S(2)}, u32[]{:S(2)}) collective-permute-start(s32[]{:T(128)} %bitcast.16), channel_id=1, source_target_pairs={{0,16},{4,20},{8,24},{12,28},{16,0},{20,4},{24,8},{28,12},{1,17},{... | collective-permute-start | bytes 20 | tf_op jit(solution)/shard_map/ppermute | solution.py:14
  128.0 3.8 copy-start.4
  128.0 3.8 copy-start.8
  163.6 193.7 %copy-start.3 = (f32[64,256]{1,0:T(8,128)}, f32[64,256]{1,0:T(8,128)S(1)}, u32[]{:S(2)}) copy-start(f32[64,256]{1,0:T(8,128)S(1)} %get-tuple-element.268) | copy-start | bytes 196612
  163.6 164.3 %collective-permute-start.3 = (f32[4,1000,256]{2,1,0:T(8,128)}, f32[4,1000,256]{2,1,0:T(8,128)}, u32[]{:S(2)}, u32[]{:S(2)}) collective-permute-start(f32[4,1000,256]{2,1,0:T(8,128)} %get-tuple-element.267), channel_id=1, source_target_pairs={{0,16},{4,20},{8,24},{12,28},{16,0},{20,4},{24,8},{28,12},{1,17},{... | collective-permute-start | bytes 12288008 | tf_op jit(solution)/shard_map/ppermute | solution.py:14
  357.2 4.7 copy-start.7
  357.3 5.8 copy-start
  384.5 155.5 %copy-start.5 = (f32[64,256]{1,0:T(8,128)S(1)}, f32[64,256]{1,0:T(8,128)}, u32[]{:S(2)}) copy-start(f32[64,256]{1,0:T(8,128)} %param.23) | copy-start | bytes 196612
  387.5 153.4 %collective-permute-start.6 = (bf16[4,1000,256]{2,1,0:T(8,128)(2,1)}, bf16[4,1000,256]{2,1,0:T(8,128)(2,1)}, u32[]{:S(2)}, u32[]{:S(2)}) collective-permute-start(bf16[4,1000,256]{2,1,0:T(8,128)(2,1)} %bitcast.25), channel_id=1, source_target_pairs={{0,8},{4,12},{8,0},{12,4},{16,24},{20,28},{24,16},{28,20},{1,9},{5... | collective-permute-start | bytes 6144008 | tf_op jit(solution)/shard_map/ppermute | solution.py:14
  401.7 139.1 %collective-permute-start.4 = (s32[]{:T(128)}, s32[]{:T(128)}, u32[]{:S(2)}, u32[]{:S(2)}) collective-permute-start(s32[]{:T(128)} %bitcast.22), channel_id=1, source_target_pairs={{0,8},{4,12},{8,0},{12,4},{16,24},{20,28},{24,16},{28,20},{1,9},{5... | collective-permute-start | bytes 20 | tf_op jit(solution)/shard_map/ppermute | solution.py:14
  401.8 389.4 %all-reduce.5.cloned.1.call-start = ((), (), s32[]{:S(2)}) async-start(), calls=%async_computation.1 | async-start | bytes 131072 | tf_op jit(solution)/shard_map/psum | solution.py:89
  401.9 138.9 %collective-permute-start.5 = (s32[4,2,1000]{2,1,0:T(2,128)S(1)}, s32[4,2,1000]{2,1,0:T(2,128)S(1)}, u32[]{:S(2)}, u32[]{:S(2)}) collective-permute-start(s32[4,2,1000]{2,1,0:T(2,128)S(1)} %pad_add_fusion.1), channel_id=1, source_target_pairs={{0,8},{4,12},{8,0},{12,4},{16,24},{20,28},{24,16},{28,20},{1,9},{5... | collective-permute-start | bytes 96008 | tf_op jit(solution)/shard_map/ppermute | solution.py:14
  547.0 244.1 %copy-start.6 = (f32[64,256]{1,0:T(8,128)S(1)}, f32[64,256]{1,0:T(8,128)}, u32[]{:S(2)}) copy-start(f32[64,256]{1,0:T(8,128)} %all-reduce.3.cloned.1.call-done) | copy-start | bytes 196612
  671.8 0.6 copy-start.2
  671.8 120.8 %collective-permute-start.7 = (f32[4,1000,256]{2,1,0:T(8,128)}, f32[4,1000,256]{2,1,0:T(8,128)}, u32[]{:S(2)}, u32[]{:S(2)}) collective-permute-start(f32[4,1000,256]{2,1,0:T(8,128)} %get-tuple-element.270), channel_id=1, source_target_pairs={{0,8},{4,12},{8,0},{12,4},{16,24},{20,28},{24,16},{28,20},{1,9},{5... | collective-permute-start | bytes 12288008 | tf_op jit(solution)/shard_map/ppermute | solution.py:14
  822.3 5.8 copy-start.1
Sparse Core Ops, SparseCore 0:
  401.9 137.9 all-reduce.2
  672.6 118.5 all-reduce.4
where the time goes:
time: 844 us; the launch traced here: 845 us
  waiting for transfers between devices  505 us (60%)
  other arithmetic  166 us (20%)
  local copies, waits for them, and re-layouts  79.8 us (9%)
  matrix products  51.8 us (6%)
  starting transfers between devices  22.1 us (3%)
  between operations  14.3 us (2%)
    psum x2, waiting for transfers between devices, on_device(): rel_total = lax.psum(rel_grad, ('dom', 'rep'))  255 us
    ppermute x8, waiting for transfers between devices, from_partner(): lax.ppermute(shard, axis, [(i, i ^ 1 << distance) for i in range(lax.axis...  250 us
    scatter-add x5, other arithmetic, serve_step(): own_grad.at[targets].add(target_grad)  63.7 us
    scatter-add x2, other arithmetic, on_device(): own_grad.at[source_index.reshape(-1)].add(returned.reshape(-1, row_width))  59 us
    gather x2, local copies, waits for them, and re-layouts, on_device(): jnp.take(own_rows, source_index.reshape(-1), axis=0)  32 us
    gather x5, local copies, waits for them, and re-layouts, serve_step(): jnp.take(own_rows, targets, axis=0)  31.7 us
    ppermute x8, starting transfers between devices, from_partner(): lax.ppermute(shard, axis, [(i, i ^ 1 << distance) for i in range(lax.axis...  22 us
    dot_general x5, matrix products, batch_terms(): jnp.dot(weights_bf, target_rows, preferred_element_type=jnp.float32)  18.8 us
  transfers between devices with their start and end apart: 10, of which 4 were waited for; matrix products, arithmetic and copies ran while one was open for 0% of the time, Pallas kernels for 0%

commit v1 on v0

v1 whole, which is shorter than its diff:
```python
import functools

import jax
import jax.numpy as jnp
from jax import lax
from jax.experimental import pallas as pl
from jax.experimental.pallas import tpu as pltpu
from jax.sharding import PartitionSpec as P

ROUNDS = 2


learn_rate = 0.1
rel_rate = 0.1

f32 = jnp.float32
bf16 = jnp.bfloat16
MIB = 1 << 20
LANES = 128
SUMS = 3
SMEM_SPEC = pl.BlockSpec(memory_space=pltpu.SMEM)
VMEM_SPEC = pl.BlockSpec(memory_space=pltpu.VMEM)
ANY_SPEC = pl.BlockSpec(memory_space=pl.ANY)
HBM_SPEC = pl.BlockSpec(memory_space=pltpu.HBM)


def from_partner(shard, axis, distance, senders=(0, 1)):
    pairs = [(i, i ^ distance) for i in range(lax.axis_size(axis)) if (i & distance != 0) in senders]
    return lax.ppermute(shard, axis, pairs)


def unroll_of(count):
    return max(d for d in range(1, 41) if count % d == 0)


def task_list(meta_ref, task, slots):
    own, theirs, low = meta_ref[0], meta_ref[1], meta_ref[2] == 1
    if isinstance(task, int) and task < 2:
        return task == 0, task * slots
    first = jnp.where(low, own, theirs) - 1
    is_first = task - 2 < first
    number = jnp.where(is_first, task - 1, task - 1 - first)
    is_own = is_first == low
    return is_own, jnp.where(is_own, number, slots + number)


def task_count(meta_ref):
    return meta_ref[0] + meta_ref[1]


def fetch_list(lists_ref, number, list_ref, sem):
    size = list_ref.shape[0]
    return pltpu.make_async_copy(lists_ref.at[pl.ds(pl.multiple_of(number * size, size), size)], list_ref, sem)


def gather_rows(batch, list_ref, table, buffer, out_ref):
    unroll = unroll_of(batch)
    halves, size, _ = buffer.shape
    if size > batch:
        buffer[:, batch:, :] = jnp.zeros((halves, size - batch, LANES), f32)

    def step(i, carry):
        at = i * unroll
        for u in range(unroll):
            row = list_ref[at + u]
            for h in range(halves):
                buffer[h, pl.ds(at + u, 1), :] = table[h, pl.ds(row, 1), :]
        return carry

    lax.fori_loop(0, batch // unroll, step, 0)
    for h in range(halves):
        out_ref[:size, h * LANES : (h + 1) * LANES] = buffer[h].astype(bf16)


def scatter_rows(batch, halves, list_ref, grads, totals):
    unroll = unroll_of(batch)

    def step(i, carry):
        at = i * unroll
        for u in range(unroll):
            row = pl.ds(pl.multiple_of(list_ref[at + u] * halves, halves), halves)
            totals[u % SUMS][row, :] += grads[pl.ds(pl.multiple_of((at + u) * halves, halves), halves), :]
        return carry

    lax.fori_loop(0, batch // unroll, step, 0)


def load_table(rows_ref, table, sems):
    return [
        pltpu.make_async_copy(rows_ref.at[:, pl.ds(h * LANES, LANES)], table.at[h], sems.at[h])
        for h in range(table.shape[0])
    ]


def load_kernel(batch, lists_ref, rows_ref, table, sent_ref, buffer, list_ref, list_sem, sems):
    copies = load_table(rows_ref, table, sems) + [fetch_list(lists_ref, 0, list_ref, list_sem)]
    for copy in copies:
        copy.start()
    for copy in copies:
        copy.wait()
    gather_rows(batch, list_ref, table, buffer, sent_ref)


def gather_kernel(batch, slots, tasks, meta_ref, lists_ref, table, *refs):
    outs, (buffer, *held, sems) = refs[: len(tasks)], refs[len(tasks) :]
    copies = [
        fetch_list(lists_ref, task_list(meta_ref, task, slots)[1], held[n], sems.at[n])
        for n, task in enumerate(tasks)
    ]
    for n, task in enumerate(tasks):
        pl.when(task < task_count(meta_ref))(copies[n].start)
    for n, task in enumerate(tasks):

        @pl.when(task < task_count(meta_ref))
        def _():
            copies[n].wait()
            gather_rows(batch, held[n], table, buffer, outs[n])


def batch_task(
    batch, live, is_own, number, kinds_ref, relations_ref, local, remote, rel_out, out_ref, left, right, weights, scale
):
    size, width = left.shape
    halves = width // LANES
    sent = local.shape[0]
    rel_count = relations_ref.shape[0]
    block = size
    inverse = 1.0 / (batch - 1)

    @pl.when(live)
    def _():
        kinds = kinds_ref[pl.ds(number, 1), :]
        full = relations_ref[...]
        high = full.astype(bf16)
        rest = full - high.astype(f32)
        middle = rest.astype(bf16)
        low = (rest - middle.astype(f32)).astype(bf16)
        kind_rows = lax.broadcasted_iota(jnp.int32, (rel_count, size), 0)
        onehot = jnp.where(kind_rows == kinds, 1.0, 0.0).astype(bf16)
        diagonal = lax.dot_general(
            jnp.concatenate([onehot, onehot, onehot], axis=0),
            jnp.concatenate([high, middle, low], axis=0),
            (((0,), (0,)), ((), ())),
            preferred_element_type=f32,
        )
        scale[...] = jnp.where(is_own, diagonal, 1.0)
        left[:sent, :] = (local[...].astype(f32) * scale[:sent, :]).astype(bf16)
        right[:sent, :] = (remote[...].astype(f32) * jnp.where(is_own, 1.0, diagonal[:sent, :])).astype(bf16)
        if size > sent:
            left[sent:, :] = jnp.zeros((size - sent, width), bf16)
            right[sent:, :] = jnp.zeros((size - sent, width), bf16)
        rel_grad = rel_out[...]
        on_diag = lax.broadcasted_iota(jnp.int32, (block, block), 0) == lax.broadcasted_iota(
            jnp.int32, (block, block), 1
        )
        for start in range(0, size, block):
            rows = pl.ds(start, block)
            scores = lax.dot_general(
                left[rows, :], right[...], (((1,), (1,)), ((), ())), preferred_element_type=f32
            )
            probs = 0.5 * jnp.tanh(0.5 * scores) + 0.5
            weights[...] = (probs * inverse).astype(bf16)
            square = probs[:, start : start + block]
            weights[:, pl.ds(start, block)] = jnp.where(on_diag, square - 1.0, square * inverse).astype(bf16)
            grads = jnp.dot(weights[...], right[...], preferred_element_type=f32)
            stop = min(start + block, sent)
            used = stop - start
            scaled = grads * scale[rows, :]
            for h in range(halves):
                out_ref[pl.ds(start * halves + h, used, stride=halves), :] = scaled[
                    :used, h * LANES : (h + 1) * LANES
                ]
            own_rows = local[start:stop, :].astype(f32)
            terms = jnp.where(is_own, grads[:used, :] * own_rows, 0.0)
            terms_high = terms.astype(bf16)
            terms_low = (terms - terms_high.astype(f32)).astype(bf16)
            kind_part = onehot[:, start:stop]
            rel_grad = (
                rel_grad
                + jnp.dot(kind_part, terms_high, preferred_element_type=f32)
                + jnp.dot(kind_part, terms_low, preferred_element_type=f32)
            )
        rel_out[...] = rel_grad


def pair_kernel(
    batch, slots, tasks, meta_ref, kinds_ref, relations_ref, local_a, local_b, remote_a, remote_b, rel_in,
    rel_out, out_a, out_b, left, right, weights, scale,
):
    rel_out[...] = rel_in[...]
    for task, mine, theirs, out_ref in ((tasks[0], local_a, remote_a, out_a), (tasks[1], local_b, remote_b, out_b)):
        is_own, number = task_list(meta_ref, task, slots)
        batch_task(
            batch, task < task_count(meta_ref), is_own, number, kinds_ref, relations_ref, mine, theirs, rel_out,
            out_ref, left, right, weights, scale,
        )


def last_kernel(batch, slots, pairs, meta_ref, kinds_ref, relations_ref, rel_in, *refs):
    mine, theirs, refs = refs[: 2 * pairs], refs[2 * pairs : 4 * pairs], refs[4 * pairs :]
    rel_out, out_a, out_b, left, right, weights, scale, local, remote, sems = refs
    rel_out[...] = rel_in[...]
    last = (task_count(meta_ref) - 1) >> 1
    tasks = [2 * last, 2 * last + 1]

    def copies(part, pair):
        return [
            pltpu.make_async_copy(mine[2 * pair + part], local.at[part], sems.at[part, 0]),
            pltpu.make_async_copy(theirs[2 * pair + part], remote.at[part], sems.at[part, 1]),
        ]

    for part, task in enumerate(tasks):
        for pair in range(pairs):

            @pl.when((task < task_count(meta_ref)) & (last == pair))
            def _():
                for copy in copies(part, pair):
                    copy.start()

    for part, (task, out_ref) in enumerate(zip(tasks, (out_a, out_b))):
        live = task < task_count(meta_ref)

        @pl.when(live)
        def _():
            for copy in copies(part, 0):
                copy.wait()

        is_own, number = task_list(meta_ref, task, slots)
        is_own = jnp.where(task < 2, task, jnp.where(is_own, 0, 1)) == 0
        number = jnp.where(task < 2, task * slots, number)
        batch_task(
            batch, live, is_own, number, kinds_ref, relations_ref, local.at[part], remote.at[part], rel_out, out_ref,
            left, right, weights, scale,
        )


def nothing_kernel(*outs):
    pass


def add_grads(batch, halves, lives, numbers, lists_ref, grads, totals, held, sems):
    copies = [fetch_list(lists_ref, number, held[n], sems.at[n]) for n, number in enumerate(numbers)]
    for live, copy in zip(lives, copies):
        pl.when(live)(copy.start)
    for n, (live, copy) in enumerate(zip(lives, copies)):

        @pl.when(live)
        def _():
            copy.wait()
            scatter_rows(batch, halves, held[n], grads[n], totals)


def add_kernel(batch, slots, halves, pair, meta_ref, lists_ref, grads_a, grads_b, *refs):
    totals, (own, sent, sems) = refs[-3 - SUMS : -3], refs[-3:]
    if pair == 0:
        for total in totals:
            total[...] = jnp.zeros_like(total)
    live = pair < (task_count(meta_ref) - 1) >> 1
    numbers = [task_list(meta_ref, 2 * pair + part, slots)[1] for part in range(2)]
    add_grads(batch, halves, (live, live), numbers, lists_ref, (grads_a, grads_b), totals, (own, sent), sems)


def add_last_kernel(batch, slots, halves, meta_ref, lists_ref, grads_a, grads_b, *refs):
    totals, (own, sent, sems) = refs[SUMS : 2 * SUMS], refs[2 * SUMS :]
    last = (task_count(meta_ref) - 1) >> 1
    tasks = [2 * last, 2 * last + 1]
    lives = [task < task_count(meta_ref) for task in tasks]
    numbers = [jnp.where(task < 2, task * slots, task_list(meta_ref, task, slots)[1]) for task in tasks]
    add_grads(batch, halves, lives, numbers, lists_ref, (grads_a, grads_b), totals, (own, sent), sems)


def update_kernel(state_ref, rows_ref, *refs):
    totals, (table, new_state, new_rows, in_sems, out_sems) = refs[:SUMS], refs[SUMS:]
    halves, count, _ = table.shape
    width = halves * LANES
    chunk = LANES
    unroll = 8
    group = unroll * chunk

    def out_copies(number):
        rows = pl.ds(pl.multiple_of(number * group, group), group)
        return [
            pltpu.make_async_copy(
                table.at[h, rows, :], new_rows.at[rows, pl.ds(h * LANES, LANES)], out_sems.at[number, h]
            )
            for h in range(halves)
        ]

    def in_copies(number):
        rows = pl.ds(pl.multiple_of(number * group, group), group)
        return [
            pltpu.make_async_copy(
                rows_ref.at[rows, pl.ds(h * LANES, LANES)], table.at[h, rows, :], in_sems.at[number, h]
            )
            for h in range(halves)
        ]

    def begin(number, carry):
        for copy in in_copies(number):
            copy.start()
        return carry

    def update_group(number, carry):
        for copy in in_copies(number):
            copy.wait()
        for u in range(unroll):
            at = number * unroll + u
            first = pl.multiple_of(at * chunk, chunk)
            rows = pl.ds(first, chunk)
            grads = [
                sum(total[pl.ds(first * halves + h, chunk, stride=halves), :] for total in totals)
                for h in range(halves)
            ]
            squares = sum(g * g for g in grads)
            mean = jnp.sum(jnp.transpose(squares), axis=0, keepdims=True) * (1.0 / width)
            now = state_ref[pl.ds(at, 1), :] + mean
            new_state[pl.ds(at, 1), :] = now
            factor = jnp.transpose(jnp.broadcast_to(learn_rate * lax.rsqrt(now), (chunk, LANES)))
            for h in range(halves):
                table[h, rows, :] = table[h, rows, :] - grads[h] * factor
        for copy in out_copies(number):
            copy.start()
        return carry

    def finish(number, carry):
        for copy in out_copies(number):
            copy.wait()
        return carry

    lax.fori_loop(0, count // group, begin, 0)
    lax.fori_loop(0, count // group, update_group, 0)
    lax.fori_loop(0, count // group, finish, 0)


def params(mib):
    return pltpu.CompilerParams(vmem_limit_bytes=mib * MIB)


def in_vmem(array):
    return pltpu.with_memory_space_constraint(array, pltpu.VMEM)


def in_hbm(array):
    return pltpu.with_memory_space_constraint(array, pltpu.HBM)


def cost(us):
    return pl.CostEstimate(flops=0, bytes_accessed=int(us * 3.4e6), transcendentals=0)


def on_device(
    embeddings, row_state, relations, rel_state, edge_src, edge_dst, edge_rel, batch_count
):
    bit_count = lax.axis_size("dom").bit_length() - 1
    row_count, width = embeddings.shape
    slots, batch = edge_src.shape[3:]
    halves = width // LANES
    size = -(-batch // 256) * 256
    sent_size = -(-batch // 16) * 16
    list_size = -(-batch // 1024) * 1024
    pairs = slots
    sent_shape = jax.ShapeDtypeStruct((sent_size, width), bf16)
    grads_shape = jax.ShapeDtypeStruct((halves * sent_size, LANES), f32)
    rel_shape = jax.ShapeDtypeStruct(relations.shape, f32)
    table_shape = pltpu.VMEM((halves, row_count, LANES), f32)
    total_shape = pltpu.VMEM((halves * row_count, LANES), f32)
    buffer = pltpu.VMEM((halves, sent_size, LANES), f32)
    one_list = pltpu.SMEM((list_size,), jnp.int32)
    dma = pltpu.SemaphoreType.DMA
    task_scratch = [
        pltpu.VMEM((size, width), bf16),
        pltpu.VMEM((size, width), bf16),
        pltpu.VMEM((size, size), bf16),
        pltpu.VMEM((size, width), f32),
    ]
    swaps = [1 << (bit_count - 1 - number) for number in range(ROUNDS)]

    def padded(ids):
        return jnp.pad(ids, ((0, 0), (0, list_size - batch)))

    state = row_state.reshape(row_count // LANES, LANES)
    sources = [padded(edge_src[0, 0, number]) for number in range(ROUNDS)]
    is_low = jnp.stack([(lax.axis_index("dom") & swap == 0).astype(jnp.int32) for swap in swaps])
    is_low, sources = lax.optimization_barrier((is_low, sources))
    table, sent = pl.pallas_call(
        functools.partial(load_kernel, batch),
        out_shape=[table_shape, sent_shape],
        in_specs=[ANY_SPEC, HBM_SPEC],
        out_specs=[VMEM_SPEC] * 2,
        scratch_shapes=[buffer, one_list, dma, dma((halves,))],
        compiler_params=params(16),
        cost_estimate=cost(5),
        name="load_and_gather",
    )(sources[0].reshape(-1), in_hbm(embeddings))
    sent, edge_dst, edge_rel, batch_count = lax.optimization_barrier((sent, edge_dst, edge_rel, batch_count))
    got_a = from_partner(sent, "dom", swaps[0])

    rounds = []
    for number in range(ROUNDS):
        count = batch_count[0, :, number]
        tail = jnp.broadcast_to(count[:, None], (1, list_size))
        mine = jnp.concatenate([padded(edge_dst[0, 0, number]), padded(edge_rel[0, 0, number]), tail], axis=0)
        theirs = from_partner(mine, "dom", swaps[number])
        lists = jnp.concatenate([sources[number], theirs[:slots]], axis=0).reshape(-1)
        kinds = jnp.concatenate([edge_rel[0, 0, number], theirs[slots : 2 * slots, :batch]], axis=0)
        kinds = jnp.pad(kinds, ((0, 0), (0, size - batch)), constant_values=-1)
        rounds.append((lists, kinds, jnp.concatenate([count, theirs[2 * slots, :1], is_low[number : number + 1]])))
    rounds = lax.optimization_barrier(rounds)

    for number in range(ROUNDS):
        swap = swaps[number]
        lists, kinds, meta = rounds[number]

        def gather(tasks, us, table):
            return pl.pallas_call(
                functools.partial(gather_kernel, batch, slots, tasks),
                out_shape=[sent_shape] * len(tasks),
                in_specs=[SMEM_SPEC, ANY_SPEC, VMEM_SPEC],
                out_specs=[VMEM_SPEC] * len(tasks),
                scratch_shapes=[buffer] + [one_list] * len(tasks) + [dma((len(tasks),))],
                compiler_params=params(16),
                cost_estimate=cost(us / 8),
                name="gather",
            )(meta, lists, in_vmem(table))

        if number > 0:
            (sent,) = gather((0,), 2, table)
            got_a = from_partner(sent, "dom", swap)
        (second,) = gather((1,), 2, table)
        got_b = from_partner(second, "dom", swap)
        table, got_a = lax.optimization_barrier((table, got_a))
        sent = [sent, second, *gather(tuple(range(2, 2 * slots)), 6, table)]
        late, sent, got_b = lax.optimization_barrier((meta, sent, got_b))
        tasks = late[0] + late[1]
        got_a, got_b = got_b, got_a

        def run_pair(pair, relations, sent, got_a, got_b, rel_grad):
            return pl.pallas_call(
                functools.partial(pair_kernel, batch, slots, (2 * pair, 2 * pair + 1)),
                out_shape=[rel_shape, grads_shape, grads_shape],
                in_specs=[SMEM_SPEC] + [VMEM_SPEC] * 7,
                out_specs=[VMEM_SPEC] * 3,
                scratch_shapes=task_scratch,
                compiler_params=params(16),
                cost_estimate=cost(6),
                name="batches",
            )(meta, kinds, relations, sent[0], sent[1], got_a, got_b, rel_grad)

        rel_grad = jnp.zeros(relations.shape, f32)
        grads, got = [], [got_a, got_b]
        for pair in range(pairs - 1):

            def go_on(both, relations, sent, got_a, got_b, rel_grad):
                next_a = from_partner(sent[2], "dom", swap)
                next_b = from_partner(sent[3], "dom", swap) if both else sent[3]
                rel_grad, grads_a, grads_b = run_pair(pair, relations, sent, got_a, got_b, rel_grad)
                return next_a, next_b, rel_grad, grads_a, grads_b

            def skip(relations, sent, got_a, got_b, rel_grad):
                next_a, next_b, grads_a, grads_b = pl.pallas_call(
                    nothing_kernel,
                    out_shape=[sent_shape] * 2 + [grads_shape] * 2,
                    out_specs=[ANY_SPEC] * 4,
                    name="nothing",
                )()
                return next_a, next_b, rel_grad, grads_a, grads_b

            got_a, got_b, rel_grad, grads_a, grads_b = lax.switch(
                jnp.clip(tasks - 2 * pair - 2, 0, 2),
                [skip, functools.partial(go_on, False), functools.partial(go_on, True)],
                relations, sent[2 * pair : 2 * pair + 4], got_a, got_b, rel_grad,
            )
            got += [got_a, got_b]
            grads.append((grads_a, grads_b))
        rel_grad, *last_grads = pl.pallas_call(
            functools.partial(last_kernel, batch, slots, pairs),
            out_shape=[rel_shape, grads_shape, grads_shape],
            in_specs=[SMEM_SPEC] + [VMEM_SPEC] * 3 + [ANY_SPEC] * (4 * pairs),
            out_specs=[VMEM_SPEC] * 3,
            scratch_shapes=task_scratch + [pltpu.VMEM((2, *sent_shape.shape), bf16)] * 2 + [dma((2, 2))],
            compiler_params=params(16),
            cost_estimate=cost(6),
            name="last_batches",
        )(meta, kinds, relations, rel_grad, *sent, *got)

        sums = [("rep", 1 << bit) for bit in range(lax.axis_size("rep").bit_length() - 1)]
        sums += [("dom", 1 << bit) for bit in range(bit_count)]
        rel_total, totals = rel_grad, None
        for step in range(max(pairs, len(sums))):
            part = from_partner(rel_total, *sums[step]) if step < len(sums) else None
            if step < pairs:
                last = step == pairs - 1
                totals = pl.pallas_call(
                    functools.partial(add_last_kernel, batch, slots, halves)
                    if last
                    else functools.partial(add_kernel, batch, slots, halves, step),
                    out_shape=[total_shape] * SUMS,
                    in_specs=[SMEM_SPEC, ANY_SPEC] + [VMEM_SPEC] * (2 + SUMS * (step > 0)),
                    out_specs=[VMEM_SPEC] * SUMS,
                    scratch_shapes=[one_list, one_list, dma((2,))],
                    input_output_aliases={4 + n: n for n in range(SUMS)} if step > 0 else {},
                    compiler_params=params(12),
                    cost_estimate=cost(4),
                    name="add_rows",
                )(meta, lists, *(last_grads if last else grads[step]), *(map(in_vmem, totals) if step > 0 else []))
            if part is not None:
                rel_total = rel_total + part
            if step < pairs:
                rel_total, totals = lax.optimization_barrier((rel_total, totals))
        table, state, embeddings = pl.pallas_call(
            update_kernel,
            out_shape=[
                table_shape,
                jax.ShapeDtypeStruct(state.shape, f32),
                pltpu.HBM(embeddings.shape, f32),
            ],
            in_specs=[VMEM_SPEC, HBM_SPEC] + [VMEM_SPEC] * SUMS,
            out_specs=[VMEM_SPEC] * 2 + [HBM_SPEC],
            scratch_shapes=[dma((row_count // (8 * LANES), halves))] * 2,
            compiler_params=params(12),
            cost_estimate=cost(8),
            name="update",
        )(state, in_hbm(embeddings), *map(in_vmem, totals))
        rel_state = rel_state + rel_total * rel_total
        relations = relations - rel_rate * rel_total / jnp.sqrt(rel_state)
    return (embeddings, state.reshape(row_count), relations, rel_state)


def solution(mesh):
    return jax.shard_map(
        on_device,
        mesh=mesh,
        in_specs=(
            P(("dom", "rep"), None),
            P(("dom", "rep")),
            P(),
            P(),
            P("dom", "rep", None, None, None),
            P("dom", "rep", None, None, None),
            P("dom", "rep", None, None, None),
            P("dom", "rep", None),
        ),
        out_specs=(P(("dom", "rep"), None), P(("dom", "rep")), P(), P()),
        check_vma=False,
    )
```

time: 844 us -> 292 us (0.35)
  waiting for transfers between devices: 505 us -> 80.6 us
  other arithmetic: 166 us -> 5.06 us
  Pallas kernels: 0 us -> 89.6 us
  local copies, waits for them, and re-layouts: 79.8 us -> 8.1 us
  starting transfers between devices: 22.1 us -> 89.1 us
  matrix products: 51.8 us -> 0 us
  loops' own time: 5.59 us -> 17.7 us
  between operations: 14.3 us -> 4.11 us
    psum x2 -> x0, waiting for transfers between devices: 255 us -> none  [on_device(): rel_total = lax.psum(rel_grad, ('dom', 'rep'))]
    ppermute x8 -> x19, waiting for transfers between devices: 250 us -> 80.6 us  [from_partner(): return lax.ppermute(shard, axis, pairs)]
    scatter-add x7 -> x0, other arithmetic: 123 us -> none  [the longest x5 63.7 us: serve_step(): own_grad.at[targets].add(target_grad)]
    pallas_call x0 -> x24, Pallas kernels: none -> 89.6 us  [the longest x8 22 us: on_device(): pl.pallas_call(functools.partial(add_last_kernel, batch, slots, halves) i...]
    ppermute x8 -> x19, starting transfers between devices: 22 us -> 89.1 us  [from_partner(): return lax.ppermute(shard, axis, pairs)]
    gather x7 -> x0, local copies, waits for them, and re-layouts: 63.7 us -> none  [the longest x2 32 us: on_device(): jnp.take(own_rows, source_index.reshape(-1), axis=0)]
    dot_general x25 -> x0, matrix products: 51.8 us -> none  [the longest x5 18.8 us: batch_terms(): jnp.dot(weights_bf, target_rows, preferred_element_type=jnp.float32)]
    another operation x12 -> x2, local copies, waits for them, and re-layouts: 12.7 us -> 0.01 us
  transfers between devices with their start and end apart: 10 -> 19, of which waited for: 4 -> 11; matrix products, arithmetic and copies ran while one was open for 0% -> 2% of each run, Pallas kernels for 0% -> 20%
where the time goes in v1:
time: 292 us; the launch traced here: 294 us
  Pallas kernels  89.6 us (31%)
  starting transfers between devices  89.1 us (31%)
  waiting for transfers between devices  80.6 us (28%)
  loops' own time  17.7 us (6%)
  local copies, waits for them, and re-layouts  8.1 us (3%)
  other arithmetic  5.06 us (2%)
  between operations  4.11 us (1%)
    ppermute x19, starting transfers between devices, from_partner(): return lax.ppermute(shard, axis, pairs)  89.1 us
    ppermute x19, waiting for transfers between devices, from_partner(): return lax.ppermute(shard, axis, pairs)  80.6 us
    pallas_call x8, Pallas kernels, on_device(): pl.pallas_call(functools.partial(add_last_kernel, batch, slots, halves) i...  22 us
    another operation x6, loops' own time, on_device(): lax.switch(jnp.clip(tasks - 2 * pair - 2, 0, 2), [skip, functools.partial...  17.7 us
    pallas_call x2, Pallas kernels, on_device(): pl.pallas_call(update_kernel, out_shape=[table_shape, jax.ShapeDtypeStruc...  17.4 us
    pallas_call x2, Pallas kernels, on_device(): pl.pallas_call(functools.partial(last_kernel, batch, slots, pairs), out_s...  16.8 us
    pallas_call x5, Pallas kernels, gather(): pl.pallas_call(functools.partial(gather_kernel, batch, slots, tasks), out...  15.6 us
    pallas_call x2, Pallas kernels, run_pair(): pl.pallas_call(functools.partial(pair_kernel, batch, slots, (2 * pair, 2...  13.1 us
  transfers between devices with their start and end apart: 19, of which 11 were waited for; matrix products, arithmetic and copies ran while one was open for 2% of the time, Pallas kernels for 20%

profile of v1, /device:TPU:6, one launch (start us, length us, event | category | flops | bytes accessed | tf_op | source)
XLA Modules:
  0.0 294.3 jit_solution(16113569415516501335)
XLA Ops:
  0.7 0.7 slice_bitcast_fusion.4
  1.4 0.1 add_convert_fusion
  1.5 4.8 %load_and_gather.1 = (f32[2,8192,128]{2,1,0:T(8,128)S(1)}, bf16[1008,256]{1,0:T(8,128)(2,1)S(1)}) custom-call(s32[4096]{0:T(1024)S(1)} %bitcast.59, f32[8192,256]{1,0:T(8,128)} %rows_ref.3), custom_call_target="tpu_custom_call" | custom-call | bytes 17000000 | tf_op jit(solution)/shard_map/load_and_gather/pallas_call | solution.py:385
  6.3 0.6 fusion.5
  6.9 0.7 pad.43.clone
  7.7 1.6 collective-permute-start.19
  9.3 0.7 pad.53.clone
  10.0 0.1 fusion.1
  10.1 2.6 collective-permute-start.18
  12.7 0.3 collective-permute-start.20
  13.0 0.6 fusion.4
  13.7 19.3 %collective-permute-done.18 = s32[9,1024]{1,0:T(8,128)S(1)} collective-permute-done((s32[9,1024]{1,0:T(8,128)S(1)}, s32[9,1024]{1,0:T(8,128)S(1)}, u32[]{:S(2)}, u32[]{:S(2)}) %collective-permute-start.18) | collective-permute-done | bytes 36896 | tf_op jit(solution)/shard_map/ppermute | solution.py:29
  33.0 0.5 slice.87
  33.6 2.0 pad_add_fusion.5.meta_ref
  35.5 0.5 slice.84
  36.0 2.0 pad_add_fusion.4.meta_ref
  38.1 2.4 gather.5.refs_1_
  40.6 3.4 %collective-permute-done.20.refs_9_ = bf16[1008,256]{1,0:T(8,128)(2,1)S(1)} collective-permute-done((bf16[1008,256]{1,0:T(8,128)(2,1)S(1)}, bf16[1008,256]{1,0:T(8,128)(2,1)S(1)}, u32[]{:S(2)}, u32[]{:S(2)}) %collective-permute-start.20) | collective-permute-done | bytes 516128 | tf_op jit(solution)/shard_map/ppermute | solution.py:29
  44.0 6.4 %gather.6 = (bf16[1008,256]{1,0:T(8,128)(2,1)}, bf16[1008,256]{1,0:T(8,128)(2,1)S(1)}, bf16[1008,256]{1,0:T(8,128)(2,1)}, bf16[1008,256]{1,0:T(8,128)(2,1)S(1)},...) custom-call(s32[3]{0:T(128)S(1)} %pad_add_fusion.4.meta_ref, s32[8192]{0:T(1024)S(1)} %bitcast.54, ...), custom_call_target="tpu_custom_call" | custom-call | bytes 2550000 | tf_op jit(solution)/shard_map/gather/pallas_call | solution.py:415
  50.4 9.7 %collective-permute-done.21.refs_8_ = bf16[1008,256]{1,0:T(8,128)(2,1)S(1)} collective-permute-done((bf16[1008,256]{1,0:T(8,128)(2,1)S(1)}, bf16[1008,256]{1,0:T(8,128)(2,1)S(1)}, u32[]{:S(2)}, u32[]{:S(2)}) %collective-permute-start.21) | collective-permute-done | bytes 516128 | tf_op jit(solution)/shard_map/ppermute | solution.py:29
  60.1 0.6 fusion.3
  62.0 27.6 %conditional.6 = (bf16[1008,256]{1,0:T(8,128)(2,1)}, bf16[1008,256]{1,0:T(8,128)(2,1)}, f32[64,256]{1,0:T(8,128)S(1)}, f32[2016,128]{1,0:T(8,128)}, f32[2016,128]{1,0:T(8,128)}) conditional(s32[]{:T(128)} %bitcast.17, () %tuple.100, (bf16[1008,256]{1,0:T(8,128)(2,1)}, s32[3]{0:T(128)S(1)}, s32[8,1024]{1,0:T(8,128)S(1)}, ...), branch_computations={%region_0.1_spmd, %region_1.2_spmd, %region_2.3_spmd} | conditional | bytes 28723252 | solution.py:468
  62.1 2.9 collective-permute-start.2
  65.0 5.8 %batches.13 = (f32[64,256]{1,0:T(8,128)S(1)}, f32[2016,128]{1,0:T(8,128)}, f32[2016,128]{1,0:T(8,128)}) custom-call(s32[3]{0:T(128)S(1)} %get-tuple-element.254.meta_ref, s32[8,1024]{1,0:T(8,128)S(1)} %get-tuple-element.255.kinds_ref, f32[64,256]{1,0:T(8,128)S(1)} %get-tuple-element.256.relations_ref, bf16[1008,256]{1,0:T(8,128)(2,1)S(1)} %get-tuple-element.257.local_a, ...), custom_call_target="tpu_custom_call" | custom-call | bytes 20400000 | tf_op jit(solution)/shard_map/cond/branch_2_fun/batches/pallas_call | solution.py:438
  70.8 12.5 %collective-permute-done.1 = bf16[1008,256]{1,0:T(8,128)(2,1)S(1)} collective-permute-done((bf16[1008,256]{1,0:T(8,128)(2,1)}, bf16[1008,256]{1,0:T(8,128)(2,1)S(1)}, u32[]{:S(2)}, u32[]{:S(2)}) %collective-permute-start.1) | collective-permute-done | bytes 516128 | tf_op jit(solution)/shard_map/cond/branch_2_fun/ppermute | solution.py:29
  83.3 5.5 %collective-permute-done.2 = bf16[1008,256]{1,0:T(8,128)(2,1)S(1)} collective-permute-done((bf16[1008,256]{1,0:T(8,128)(2,1)S(1)}, bf16[1008,256]{1,0:T(8,128)(2,1)S(1)}, u32[]{:S(2)}, u32[]{:S(2)}) %collective-permute-start.2) | collective-permute-done | bytes 516128 | tf_op jit(solution)/shard_map/cond/branch_2_fun/ppermute | solution.py:29
  88.8 0.8 copy-done.3
  89.6 28.4 %conditional.7 = (bf16[1008,256]{1,0:T(8,128)(2,1)}, bf16[1008,256]{1,0:T(8,128)(2,1)}, f32[64,256]{1,0:T(8,128)S(1)}, f32[2016,128]{1,0:T(8,128)}, f32[2016,128]{1,0:T(8,128)}) conditional(s32[]{:T(128)} %bitcast.16, f32[64,256]{1,0:T(8,128)S(1)} %get-tuple-element.590, (bf16[1008,256]{1,0:T(8,128)(2,1)}, s32[3]{0:T(128)S(1)}, ...), branch_computations={%region_3.4_spmd, %region_4.5_spmd, %region_5.6_spmd} | conditional | bytes 28788784 | solution.py:468
  89.6 0.8 copy.60
  90.4 7.3 %batches.14 = (f32[64,256]{1,0:T(8,128)S(1)}, f32[2016,128]{1,0:T(8,128)}, f32[2016,128]{1,0:T(8,128)}) custom-call(s32[3]{0:T(128)S(1)} %get-tuple-element.270.meta_ref, s32[8,1024]{1,0:T(8,128)S(1)} %get-tuple-element.271.kinds_ref, f32[64,256]{1,0:T(8,128)S(1)} %get-tuple-element.272.relations_ref, bf16[1008,256]{1,0:T(8,128)(2,1)} %get-tuple-element.273.local_a, ...), custom_call_target="tpu_custom_call" | custom-call | bytes 20400000 | tf_op jit(solution)/shard_map/cond/branch_1_fun/batches/pallas_call | solution.py:438
  97.7 11.5 %collective-permute-done.3 = bf16[1008,256]{1,0:T(8,128)(2,1)S(1)} collective-permute-done((bf16[1008,256]{1,0:T(8,128)(2,1)}, bf16[1008,256]{1,0:T(8,128)(2,1)S(1)}, u32[]{:S(2)}, u32[]{:S(2)}) %collective-permute-start.3) | collective-permute-done | bytes 516128 | tf_op jit(solution)/shard_map/cond/branch_1_fun/ppermute | solution.py:29
  109.2 0.8 copy-done.7
  118.0 10.0 %last_batches.2 = (f32[64,256]{1,0:T(8,128)S(1)}, f32[2016,128]{1,0:T(8,128)S(1)}, f32[2016,128]{1,0:T(8,128)S(1)}) custom-call(s32[3]{0:T(128)S(1)} %pad_add_fusion.4.meta_ref, s32[8,1024]{1,0:T(8,128)S(1)} %pad.30.kinds_ref, f32[64,256]{1,0:T(8,128)S(1)} %copy-done.13, f32[64,256]{1,0:T(8,128)S(1)} %get-tuple-element.600.rel_in, ...), custom_call_target="tpu_custom_call" | custom-call | bytes 20400000 | tf_op jit(solution)/shard_map/last_batches/pallas_call | solution.py:475
  128.1 5.7 %add_rows.8 = (f32[16384,128]{1,0:T(8,128)S(1)}, f32[16384,128]{1,0:T(8,128)S(1)}, f32[16384,128]{1,0:T(8,128)S(1)}) custom-call(s32[3]{0:T(128)S(1)} %pad_add_fusion.4.meta_ref, s32[8192]{0:T(1024)S(1)} %bitcast.55, f32[2016,128]{1,0:T(8,128)S(1)} %copy-done.14, f32[2016,128]{1,0:T(8,128)S(1)} %copy-done.15), custom_call_target="tpu_custom_call" | custom-call | bytes 13600000 | tf_op jit(solution)/shard_map/add_rows/pallas_call | solution.py:493
  134.0 4.7 %add_rows.9 = (f32[16384,128]{1,0:T(8,128)S(1)}, f32[16384,128]{1,0:T(8,128)S(1)}, f32[16384,128]{1,0:T(8,128)S(1)}) custom-call(s32[3]{0:T(128)S(1)} %pad_add_fusion.4.meta_ref, s32[8192]{0:T(1024)S(1)} %bitcast.56, f32[2016,128]{1,0:T(8,128)S(1)} %copy-done.18, ...), custom_call_target="tpu_custom_call", output_to_operand_aliasing={{0}: (4, {}), {1}: (5, {}), {2}: (6, {})} | custom-call | bytes 13600000 | tf_op jit(solution)/shard_map/add_rows/pallas_call | solution.py:493
  138.8 0.6 add_rows.10
  139.4 3.6 %collective-permute-done.24 = f32[64,256]{1,0:T(8,128)S(1)} collective-permute-done((f32[64,256]{1,0:T(8,128)S(1)}, f32[64,256]{1,0:T(8,128)S(1)}, u32[]{:S(2)}, u32[]{:S(2)}) %collective-permute-start.24) | collective-permute-done | bytes 65568 | tf_op jit(solution)/shard_map/ppermute | solution.py:29
  143.1 6.7 %collective-permute-start.25 = (f32[64,256]{1,0:T(8,128)S(1)}, f32[64,256]{1,0:T(8,128)S(1)}, u32[]{:S(2)}, u32[]{:S(2)}) collective-permute-start(f32[64,256]{1,0:T(8,128)S(1)} %add.85), channel_id=1, source_target_pairs={{0,8},{4,12},{8,0},{12,4},{16,24},{20,28},{24,16},{28,20},{1,9},{5... | collective-permute-start | bytes 196616 | tf_op jit(solution)/shard_map/ppermute | solution.py:29
  149.8 2.9 add_rows.11
  152.8 7.0 %update.2 = (f32[2,8192,128]{2,1,0:T(8,128)S(1)}, f32[64,128]{1,0:T(8,128)S(1)}, f32[8192,256]{1,0:T(8,128)}) custom-call(f32[64,128]{1,0:T(8,128)S(1)} %bitcast.60, f32[8192,256]{1,0:T(8,128)} %rows_ref.3, f32[16384,128]{1,0:T(8,128)S(1)} %get-tuple-element.636.refs_0_, f32[16384,128]{1,0:T(8,128)S(1)} %get-tuple-element.637.refs_1_, ...), custom_call_target="tpu_custom_call" | custom-call | bytes 27200000 | tf_op jit(solution)/shard_map/update/pallas_call | solution.py:510
  159.9 2.4 gather.7.refs_0_
  162.3 1.9 collective-permute-start.27
  164.2 2.4 gather.8.refs_1_
  166.6 0.3 collective-permute-start.28
  166.8 2.9 collective-permute-start.26
  169.8 11.7 %collective-permute-done.26 = f32[64,256]{1,0:T(8,128)S(1)} collective-permute-done((f32[64,256]{1,0:T(8,128)S(1)}, f32[64,256]{1,0:T(8,128)S(1)}, u32[]{:S(2)}, u32[]{:S(2)}) %collective-permute-start.26) | collective-permute-done | bytes 65568 | tf_op jit(solution)/shard_map/ppermute | solution.py:29
  181.4 2.0 gather.9
  183.4 0.1 collective-permute-done.28.refs_8_
  183.6 0.6 fusion.2
  185.5 0.2 conditional.9
  185.8 9.4 %conditional.11 = (bf16[1008,256]{1,0:T(8,128)(2,1)}, bf16[1008,256]{1,0:T(8,128)(2,1)}, f32[64,256]{1,0:T(8,128)S(1)}, f32[2016,128]{1,0:T(8,128)}, f32[2016,128]{1,0:T(8,128)}) conditional(s32[]{:T(128)} %bitcast.18, f32[64,256]{1,0:T(8,128)S(1)} %get-tuple-element.665, (bf16[1008,256]{1,0:T(8,128)(2,1)}, s32[3]{0:T(128)S(1)}, ...), branch_computations={%region_15.16_spmd, %region_16.17_spmd, %region_17.18_spmd} | conditional | bytes 28788784 | solution.py:468
  195.2 6.8 %last_batches.3 = (f32[64,256]{1,0:T(8,128)S(1)}, f32[2016,128]{1,0:T(8,128)S(1)}, f32[2016,128]{1,0:T(8,128)S(1)}) custom-call(s32[3]{0:T(128)S(1)} %pad_add_fusion.5.meta_ref, s32[8,1024]{1,0:T(8,128)S(1)} %pad.33.kinds_ref, f32[64,256]{1,0:T(8,128)S(1)} %multiply_subtract_fusion.1.relations_ref, f32[64,256]{1,0:T(8,128)S(1)} %get-tuple-element.670.rel_in, ...), custom_call_target="tpu_custom_call" | custom-call | bytes 20400000 | tf_op jit(solution)/shard_map/last_batches/pallas_call | solution.py:475
  202.1 2.2 add_rows.12
  204.4 21.1 %collective-permute-start.30 = (f32[64,256]{1,0:T(8,128)S(1)}, f32[64,256]{1,0:T(8,128)S(1)}, u32[]{:S(2)}, u32[]{:S(2)}) collective-permute-start(f32[64,256]{1,0:T(8,128)S(1)} %add.90), channel_id=1, source_target_pairs={{0,2},{1,3},{2,0},{3,1},{4,6},{5,7},{6,4},{7,5},{8,10},{9,11},{10,... | collective-permute-start | bytes 196616 | tf_op jit(solution)/shard_map/ppermute | solution.py:29
  225.5 0.6 add_rows.13
  226.1 1.6 collective-permute-done.30
  227.7 13.6 %collective-permute-start.31 = (f32[64,256]{1,0:T(8,128)S(1)}, f32[64,256]{1,0:T(8,128)S(1)}, u32[]{:S(2)}, u32[]{:S(2)}) collective-permute-start(f32[64,256]{1,0:T(8,128)S(1)} %add.91), channel_id=1, source_target_pairs={{0,4},{4,0},{8,12},{12,8},{16,20},{20,16},{24,28},{28,24},{1,5},{5... | collective-permute-start | bytes 196616 | tf_op jit(solution)/shard_map/ppermute | solution.py:29
  241.3 0.6 add_rows.14
  241.9 1.7 collective-permute-done.31
  243.6 1.2 collective-permute-start.32
  244.8 4.7 %add_rows.15 = (f32[16384,128]{1,0:T(8,128)S(1)}, f32[16384,128]{1,0:T(8,128)S(1)}, f32[16384,128]{1,0:T(8,128)S(1)}) custom-call(s32[3]{0:T(128)S(1)} %pad_add_fusion.5.meta_ref, s32[8192]{0:T(1024)S(1)} %bitcast.52, f32[2016,128]{1,0:T(8,128)S(1)} %get-tuple-element.698.grads_a, ...), custom_call_target="tpu_custom_call", output_to_operand_aliasing={{0}: (4, {}), {1}: (5, {}), {2}: (6, {})} | custom-call | bytes 13600000 | tf_op jit(solution)/shard_map/add_rows/pallas_call | solution.py:493
  249.6 33.5 %collective-permute-start.33 = (f32[64,256]{1,0:T(8,128)S(1)}, f32[64,256]{1,0:T(8,128)S(1)}, u32[]{:S(2)}, u32[]{:S(2)}) collective-permute-start(f32[64,256]{1,0:T(8,128)S(1)} %add.93), channel_id=1, source_target_pairs={{0,16},{4,20},{8,24},{12,28},{16,0},{20,4},{24,8},{28,12},{1,17},{... | collective-permute-start | bytes 196616 | tf_op jit(solution)/shard_map/ppermute | solution.py:29
  283.1 10.3 %update.3 = (f32[2,8192,128]{2,1,0:T(8,128)}, f32[64,128]{1,0:T(8,128)}, f32[8192,256]{1,0:T(8,128)}) custom-call(f32[64,128]{1,0:T(8,128)S(1)} %get-tuple-element.639.state_ref, f32[8192,256]{1,0:T(8,128)} %get-tuple-element.640.rows_ref, f32[16384,128]{1,0:T(8,128)S(1)} %get-tuple-element.706.refs_0_, f32[16384,128]{1,0:T(8,128)S(1)} %get-tuple-element.707.refs_1_, ...), custom_call_target="tpu_custom_call" | custom-call | bytes 27200000 | tf_op jit(solution)/shard_map/update/pallas_call | solution.py:510
  293.4 0.7 multiply_subtract_fusion
  (90 shorter events, 0.9 us)
Async XLA Ops:
  0.6 5.7 %copy-start.35 = (s32[1,1,2]{2,1,0:T(1,128)S(1)}, s32[1,1,2]{2,1,0:T(1,128)}, u32[]{:S(2)}) copy-start(s32[1,1,2]{2,1,0:T(1,128)} %param.33) | copy-start | bytes 28
  0.6 7.0 %copy-start.33 = (s32[1,1,2,4,1000]{4,3,2,1,0:T(4,128)S(1)}, s32[1,1,2,4,1000]{4,3,2,1,0:T(4,128)}, u32[]{:S(2)}) copy-start(s32[1,1,2,4,1000]{4,3,2,1,0:T(4,128)} %param.32) | copy-start | bytes 96004
  0.7 6.9 %copy-start.34 = (s32[1,1,2,4,1000]{4,3,2,1,0:T(4,128)S(1)}, s32[1,1,2,4,1000]{4,3,2,1,0:T(4,128)}, u32[]{:S(2)}) copy-start(s32[1,1,2,4,1000]{4,3,2,1,0:T(4,128)} %param.31) | copy-start | bytes 96004
  7.7 5.9 %collective-permute-start.19 = (s32[9,1024]{1,0:T(8,128)S(1)}, s32[9,1024]{1,0:T(8,128)S(1)}, u32[]{:S(2)}, u32[]{:S(2)}) collective-permute-start(s32[9,1024]{1,0:T(8,128)S(1)} %fusion), channel_id=1, source_target_pairs={{0,8},{4,12},{8,0},{12,4},{16,24},{20,28},{24,16},{28,20},{1,9},{5... | collective-permute-start | bytes 110600 | tf_op jit(solution)/shard_map/ppermute | solution.py:29
  10.1 22.9 %collective-permute-start.18 = (s32[9,1024]{1,0:T(8,128)S(1)}, s32[9,1024]{1,0:T(8,128)S(1)}, u32[]{:S(2)}, u32[]{:S(2)}) collective-permute-start(s32[9,1024]{1,0:T(8,128)S(1)} %fusion.1), channel_id=1, source_target_pairs={{0,16},{4,20},{8,24},{12,28},{16,0},{20,4},{24,8},{28,12},{1,17},{... | collective-permute-start | bytes 110600 | tf_op jit(solution)/shard_map/ppermute | solution.py:29
  12.7 31.3 %collective-permute-start.20 = (bf16[1008,256]{1,0:T(8,128)(2,1)S(1)}, bf16[1008,256]{1,0:T(8,128)(2,1)S(1)}, u32[]{:S(2)}, u32[]{:S(2)}) collective-permute-start(bf16[1008,256]{1,0:T(8,128)(2,1)S(1)} %get-tuple-element.585.refs_0_), channel_id=1, source_target_pairs={{0,16},{4,20},{8,24},{12,28},{16,0},{20,4},{24,8},{28,12},{1,17},{... | collective-permute-start | bytes 1548296 | tf_op jit(solution)/shard_map/ppermute | solution.py:29
  38.1 23.9 %copy-start.13 = (f32[64,256]{1,0:T(8,128)S(1)}, f32[64,256]{1,0:T(8,128)}, u32[]{:S(2)}) copy-start(f32[64,256]{1,0:T(8,128)} %relations_ref.1) | copy-start | bytes 196612
  40.5 19.6 %collective-permute-start.21 = (bf16[1008,256]{1,0:T(8,128)(2,1)S(1)}, bf16[1008,256]{1,0:T(8,128)(2,1)S(1)}, u32[]{:S(2)}, u32[]{:S(2)}) collective-permute-start(bf16[1008,256]{1,0:T(8,128)(2,1)S(1)} %gather.5.refs_1_), channel_id=1, source_target_pairs={{0,16},{4,20},{8,24},{12,28},{16,0},{20,4},{24,8},{28,12},{1,17},{... | collective-permute-start | bytes 1548296 | tf_op jit(solution)/shard_map/ppermute | solution.py:29
  62.0 21.3 %collective-permute-start.1 = (bf16[1008,256]{1,0:T(8,128)(2,1)}, bf16[1008,256]{1,0:T(8,128)(2,1)S(1)}, u32[]{:S(2)}, u32[]{:S(2)}) collective-permute-start(bf16[1008,256]{1,0:T(8,128)(2,1)} %get-tuple-element.252), channel_id=1, source_target_pairs={{0,16},{4,20},{8,24},{12,28},{16,0},{20,4},{24,8},{28,12},{1,17},{... | collective-permute-start | bytes 1548296 | tf_op jit(solution)/shard_map/cond/branch_2_fun/ppermute | solution.py:29
  62.1 26.7 %collective-permute-start.2 = (bf16[1008,256]{1,0:T(8,128)(2,1)S(1)}, bf16[1008,256]{1,0:T(8,128)(2,1)S(1)}, u32[]{:S(2)}, u32[]{:S(2)}) collective-permute-start(bf16[1008,256]{1,0:T(8,128)(2,1)S(1)} %get-tuple-element.253), channel_id=1, source_target_pairs={{0,16},{4,20},{8,24},{12,28},{16,0},{20,4},{24,8},{28,12},{1,17},{... | collective-permute-start | bytes 1548296 | tf_op jit(solution)/shard_map/cond/branch_2_fun/ppermute | solution.py:29
  83.3 5.5 %copy-start.2 = (bf16[1008,256]{1,0:T(8,128)(2,1)}, bf16[1008,256]{1,0:T(8,128)(2,1)S(1)}, u32[]{:S(2)}) copy-start(bf16[1008,256]{1,0:T(8,128)(2,1)S(1)} %collective-permute-done.1) | copy-start | bytes 1548292 | tf_op jit(solution)/shard_map/cond
  88.8 0.8 copy-start.3
  89.6 19.6 %collective-permute-start.3 = (bf16[1008,256]{1,0:T(8,128)(2,1)}, bf16[1008,256]{1,0:T(8,128)(2,1)S(1)}, u32[]{:S(2)}, u32[]{:S(2)}) collective-permute-start(bf16[1008,256]{1,0:T(8,128)(2,1)} %get-tuple-element.268), channel_id=1, source_target_pairs={{0,16},{4,20},{8,24},{12,28},{16,0},{20,4},{24,8},{28,12},{1,17},{... | collective-permute-start | bytes 1548296 | tf_op jit(solution)/shard_map/cond/branch_1_fun/ppermute | solution.py:29
  109.2 0.8 copy-start.7
  118.0 10.1 %copy-start.14 = (f32[2016,128]{1,0:T(8,128)S(1)}, f32[2016,128]{1,0:T(8,128)}, u32[]{:S(2)}) copy-start(f32[2016,128]{1,0:T(8,128)} %get-tuple-element.604.grads_a) | copy-start | bytes 3096580
  118.0 10.1 %copy-start.15 = (f32[2016,128]{1,0:T(8,128)S(1)}, f32[2016,128]{1,0:T(8,128)}, u32[]{:S(2)}) copy-start(f32[2016,128]{1,0:T(8,128)} %get-tuple-element.605.grads_b) | copy-start | bytes 3096580
  118.0 15.9 %copy-start.18 = (f32[2016,128]{1,0:T(8,128)S(1)}, f32[2016,128]{1,0:T(8,128)}, u32[]{:S(2)}) copy-start(f32[2016,128]{1,0:T(8,128)} %get-tuple-element.610.grads_a) | copy-start | bytes 3096580
  118.0 15.9 %copy-start.19 = (f32[2016,128]{1,0:T(8,128)S(1)}, f32[2016,128]{1,0:T(8,128)}, u32[]{:S(2)}) copy-start(f32[2016,128]{1,0:T(8,128)} %get-tuple-element.611.grads_b) | copy-start | bytes 3096580
  128.0 5.8 %collective-permute-start.22 = (f32[64,256]{1,0:T(8,128)S(1)}, f32[64,256]{1,0:T(8,128)S(1)}, u32[]{:S(2)}, u32[]{:S(2)}) collective-permute-start(f32[64,256]{1,0:T(8,128)S(1)} %get-tuple-element.603), channel_id=1, source_target_pairs={{0,1},{1,0},{2,3},{3,2},{4,5},{5,4},{6,7},{7,6},{8,9},{9,8},{10,11... | collective-permute-start | bytes 196616 | tf_op jit(solution)/shard_map/ppermute | solution.py:29
  133.9 4.8 %collective-permute-start.23 = (f32[64,256]{1,0:T(8,128)S(1)}, f32[64,256]{1,0:T(8,128)S(1)}, u32[]{:S(2)}, u32[]{:S(2)}) collective-permute-start(f32[64,256]{1,0:T(8,128)S(1)} %add.83), channel_id=1, source_target_pairs={{0,2},{1,3},{2,0},{3,1},{4,6},{5,7},{6,4},{7,5},{8,10},{9,11},{10,... | collective-permute-start | bytes 196616 | tf_op jit(solution)/shard_map/ppermute | solution.py:29
  134.0 4.8 %copy-start.20 = (f32[2016,128]{1,0:T(8,128)S(1)}, f32[2016,128]{1,0:T(8,128)}, u32[]{:S(2)}) copy-start(f32[2016,128]{1,0:T(8,128)} %get-tuple-element.619.grads_a) | copy-start | bytes 3096580
  134.0 4.8 %copy-start.21 = (f32[2016,128]{1,0:T(8,128)S(1)}, f32[2016,128]{1,0:T(8,128)}, u32[]{:S(2)}) copy-start(f32[2016,128]{1,0:T(8,128)} %get-tuple-element.620.grads_b) | copy-start | bytes 3096580
  138.7 4.3 %collective-permute-start.24 = (f32[64,256]{1,0:T(8,128)S(1)}, f32[64,256]{1,0:T(8,128)S(1)}, u32[]{:S(2)}, u32[]{:S(2)}) collective-permute-start(f32[64,256]{1,0:T(8,128)S(1)} %add.84), channel_id=1, source_target_pairs={{0,4},{4,0},{8,12},{12,8},{16,20},{20,16},{24,28},{28,24},{1,5},{5... | collective-permute-start | bytes 196616 | tf_op jit(solution)/shard_map/ppermute | solution.py:29
  143.1 9.7 %collective-permute-start.25 = (f32[64,256]{1,0:T(8,128)S(1)}, f32[64,256]{1,0:T(8,128)S(1)}, u32[]{:S(2)}, u32[]{:S(2)}) collective-permute-start(f32[64,256]{1,0:T(8,128)S(1)} %add.85), channel_id=1, source_target_pairs={{0,8},{4,12},{8,0},{12,4},{16,24},{20,28},{24,16},{28,20},{1,9},{5... | collective-permute-start | bytes 196616 | tf_op jit(solution)/shard_map/ppermute | solution.py:29
  149.8 3.0 %copy-start = (f32[8192]{0:T(1024)S(1)}, f32[8192]{0:T(1024)}, u32[]{:S(2)}) copy-start(f32[8192]{0:T(1024)} %param.27) | copy-start | bytes 98308
  159.8 21.6 %copy-start.32 = (f32[64,256]{1,0:T(8,128)S(1)}, f32[64,256]{1,0:T(8,128)}, u32[]{:S(2)}) copy-start(f32[64,256]{1,0:T(8,128)} %param.29) | copy-start | bytes 196612
  162.3 19.2 %collective-permute-start.27 = (bf16[1008,256]{1,0:T(8,128)(2,1)S(1)}, bf16[1008,256]{1,0:T(8,128)(2,1)S(1)}, u32[]{:S(2)}, u32[]{:S(2)}) collective-permute-start(bf16[1008,256]{1,0:T(8,128)(2,1)S(1)} %gather.7.refs_0_), channel_id=1, source_target_pairs={{0,8},{4,12},{8,0},{12,4},{16,24},{20,28},{24,16},{28,20},{1,9},{5... | collective-permute-start | bytes 1548296 | tf_op jit(solution)/shard_map/ppermute | solution.py:29
  166.6 17.0 %collective-permute-start.28 = (bf16[1008,256]{1,0:T(8,128)(2,1)S(1)}, bf16[1008,256]{1,0:T(8,128)(2,1)S(1)}, u32[]{:S(2)}, u32[]{:S(2)}) collective-permute-start(bf16[1008,256]{1,0:T(8,128)(2,1)S(1)} %gather.8.refs_1_), channel_id=1, source_target_pairs={{0,8},{4,12},{8,0},{12,4},{16,24},{20,28},{24,16},{28,20},{1,9},{5... | collective-permute-start | bytes 1548296 | tf_op jit(solution)/shard_map/ppermute | solution.py:29
  166.8 14.6 %collective-permute-start.26 = (f32[64,256]{1,0:T(8,128)S(1)}, f32[64,256]{1,0:T(8,128)S(1)}, u32[]{:S(2)}, u32[]{:S(2)}) collective-permute-start(f32[64,256]{1,0:T(8,128)S(1)} %add.86), channel_id=1, source_target_pairs={{0,16},{4,20},{8,24},{12,28},{16,0},{20,4},{24,8},{28,12},{1,17},{... | collective-permute-start | bytes 196616 | tf_op jit(solution)/shard_map/ppermute | solution.py:29
  195.2 6.9 %copy-start.16 = (f32[2016,128]{1,0:T(8,128)S(1)}, f32[2016,128]{1,0:T(8,128)}, u32[]{:S(2)}) copy-start(f32[2016,128]{1,0:T(8,128)} %get-tuple-element.674.grads_a) | copy-start | bytes 3096580
  195.2 6.9 %copy-start.17 = (f32[2016,128]{1,0:T(8,128)S(1)}, f32[2016,128]{1,0:T(8,128)}, u32[]{:S(2)}) copy-start(f32[2016,128]{1,0:T(8,128)} %get-tuple-element.675.grads_b) | copy-start | bytes 3096580
  195.2 30.3 %copy-start.22 = (f32[2016,128]{1,0:T(8,128)S(1)}, f32[2016,128]{1,0:T(8,128)}, u32[]{:S(2)}) copy-start(f32[2016,128]{1,0:T(8,128)} %get-tuple-element.680.grads_a) | copy-start | bytes 3096580
  195.2 30.3 %copy-start.23 = (f32[2016,128]{1,0:T(8,128)S(1)}, f32[2016,128]{1,0:T(8,128)}, u32[]{:S(2)}) copy-start(f32[2016,128]{1,0:T(8,128)} %get-tuple-element.681.grads_b) | copy-start | bytes 3096580
  202.0 2.3 collective-permute-start.29
  204.4 23.4 %collective-permute-start.30 = (f32[64,256]{1,0:T(8,128)S(1)}, f32[64,256]{1,0:T(8,128)S(1)}, u32[]{:S(2)}, u32[]{:S(2)}) collective-permute-start(f32[64,256]{1,0:T(8,128)S(1)} %add.90), channel_id=1, source_target_pairs={{0,2},{1,3},{2,0},{3,1},{4,6},{5,7},{6,4},{7,5},{8,10},{9,11},{10,... | collective-permute-start | bytes 196616 | tf_op jit(solution)/shard_map/ppermute | solution.py:29
  225.5 15.8 %copy-start.24 = (f32[2016,128]{1,0:T(8,128)S(1)}, f32[2016,128]{1,0:T(8,128)}, u32[]{:S(2)}) copy-start(f32[2016,128]{1,0:T(8,128)} %get-tuple-element.689.grads_a) | copy-start | bytes 3096580
  225.5 15.8 %copy-start.25 = (f32[2016,128]{1,0:T(8,128)S(1)}, f32[2016,128]{1,0:T(8,128)}, u32[]{:S(2)}) copy-start(f32[2016,128]{1,0:T(8,128)} %get-tuple-element.690.grads_b) | copy-start | bytes 3096580
  227.7 15.8 %collective-permute-start.31 = (f32[64,256]{1,0:T(8,128)S(1)}, f32[64,256]{1,0:T(8,128)S(1)}, u32[]{:S(2)}, u32[]{:S(2)}) collective-permute-start(f32[64,256]{1,0:T(8,128)S(1)} %add.91), channel_id=1, source_target_pairs={{0,4},{4,0},{8,12},{12,8},{16,20},{20,16},{24,28},{28,24},{1,5},{5... | collective-permute-start | bytes 196616 | tf_op jit(solution)/shard_map/ppermute | solution.py:29
  243.6 6.0 %collective-permute-start.32 = (f32[64,256]{1,0:T(8,128)S(1)}, f32[64,256]{1,0:T(8,128)S(1)}, u32[]{:S(2)}, u32[]{:S(2)}) collective-permute-start(f32[64,256]{1,0:T(8,128)S(1)} %add.92), channel_id=1, source_target_pairs={{0,8},{4,12},{8,0},{12,4},{16,24},{20,28},{24,16},{28,20},{1,9},{5... | collective-permute-start | bytes 196616 | tf_op jit(solution)/shard_map/ppermute | solution.py:29
  249.6 43.8 %collective-permute-start.33 = (f32[64,256]{1,0:T(8,128)S(1)}, f32[64,256]{1,0:T(8,128)S(1)}, u32[]{:S(2)}, u32[]{:S(2)}) collective-permute-start(f32[64,256]{1,0:T(8,128)S(1)} %add.93), channel_id=1, source_target_pairs={{0,16},{4,20},{8,24},{12,28},{16,0},{20,4},{24,8},{28,12},{1,17},{... | collective-permute-start | bytes 196616 | tf_op jit(solution)/shard_map/ppermute | solution.py:29
